TPU v7x, 32 devices: a whole 2x2x4 slice. The times are simulated.
32 devices in a mesh: lon: 8 (over y, x, core), lat: 4 (over z).
Axes of the slice: x: 2, y: 2, z: 4, core: 2. Of those that a mesh axis runs over, the one named last changes fastest.
Arguments:
- fields: bfloat16 [2, 96, 192, 512], P(None, 'lat', 'lon'), may hold values from -6 to 6
- cotangent: bfloat16 [2, 96, 192, 512], P(None, 'lat', 'lon'), may hold values from -6 to 6
- qkv_weight: bfloat16 [512, 1536], replicated, may hold values from -1 to 1, as said below
- out_weight: bfloat16 [512, 512], replicated, may hold values from -0.25 to 0.25
Outputs:
- output_field: bfloat16 [2, 96, 192, 512], P(None, 'lat', 'lon')
- field_grad: bfloat16 [2, 96, 192, 512], P(None, 'lat', 'lon')
- qkv_grad: float32 [512, 1536], P(('lon', 'lat'))
- out_grad: float32 [512, 512], P(('lon', 'lat'))
Inputs may be any that keep to these rules, and one draw needn't show every extreme that they name: `qkv_weight`: a dense projection matrix, about 512^-0.5 in scale.
All inputs are finite; a program needn't handle non-finite values.
Results may differ from a plain program's by a relative error of at most 0.015.
Values may be sent and summed in bfloat16 or wider, within the bound.
No kernel may reach another device: no remote copies, remote signals or barrier semaphores. Data moves between devices by JAX's collectives and lax.ppermute only.
A program may use at most 192 MiB of HBM per device.

v0:
```python
import jax
import jax.numpy as jnp
from jax import lax
from jax.sharding import PartitionSpec as P

HEADS = 16
WIN_LAT = 6
WIN_LON = 12


def from_behind(x, axis, by):
    length = lax.axis_size(axis)
    return lax.ppermute(x, axis, [(i, (i + by) % length) for i in range(length)])


def normalize(values):
    center = jnp.mean(values, axis=-1, keepdims=True)
    centred = values - center
    spread = jnp.mean(centred * centred, axis=-1, keepdims=True)
    return centred * lax.rsqrt(spread + 1e-05)


def attend(projected, groups):
    wincount, tokens_win, triple = projected.shape
    width = triple // 3
    head_size = width // HEADS
    queries = projected[..., :width].reshape(wincount, tokens_win, HEADS, head_size)
    keyset = projected[..., width : 2 * width].reshape(wincount, tokens_win, HEADS, head_size)
    valueset = projected[..., 2 * width :].reshape(wincount, tokens_win, HEADS, head_size)
    scores = jnp.einsum(
        "wqhe,wkhe->whqk", queries, keyset, preferred_element_type=jnp.float32
    ) * head_size ** (-0.5)
    allowed = (groups[:, :, None] == groups[:, None, :])[:, None]
    scores = jnp.where(allowed, scores, -1000000000.0)
    highest = jnp.max(scores, axis=-1, keepdims=True)
    raised = jnp.exp(scores - highest)
    soft_weights = (raised / jnp.sum(raised, axis=-1, keepdims=True)).astype(jnp.bfloat16)
    mixture = jnp.einsum(
        "whqk,wkhe->wqhe", soft_weights, valueset, preferred_element_type=jnp.float32
    )
    return mixture.reshape(wincount, tokens_win, width).astype(jnp.bfloat16)


def to_windows(grid):
    levels, lat_cells, lon_cells, channels = grid.shape
    shaped = grid.reshape(
        levels, lat_cells // WIN_LAT, WIN_LAT, lon_cells // WIN_LON, WIN_LON, channels
    )
    shaped = shaped.transpose(1, 3, 0, 2, 4, 5)
    return shaped.reshape(
        lat_cells // WIN_LAT * (lon_cells // WIN_LON), levels * WIN_LAT * WIN_LON, channels
    )


def from_windows(windows, levels, lat_cells, lon_cells):
    channels = windows.shape[-1]
    shaped = windows.reshape(
        lat_cells // WIN_LAT, lon_cells // WIN_LON, levels, WIN_LAT, WIN_LON, channels
    )
    shaped = shaped.transpose(2, 0, 3, 1, 4, 5)
    return shaped.reshape(levels, lat_cells, lon_cells, channels)


def roll_grid(field, direction):
    shift_lat = WIN_LAT // 2
    shift_lon = WIN_LON // 2
    cutoff = shift_lat if direction < 0 else field.shape[1] - shift_lat
    leading, trailing = (field[:, :cutoff], field[:, cutoff:])
    outgoing = leading if direction < 0 else trailing
    incoming = from_behind(outgoing, "lat", direction)
    field = jnp.concatenate([trailing, incoming] if direction < 0 else [incoming, leading], axis=1)
    cutoff = shift_lon if direction < 0 else field.shape[2] - shift_lon
    leading, trailing = (field[:, :, :cutoff], field[:, :, cutoff:])
    outgoing = leading if direction < 0 else trailing
    incoming = from_behind(outgoing, "lon", direction)
    return jnp.concatenate([trailing, incoming] if direction < 0 else [incoming, leading], axis=2)


def shards(fields, cotangent, qkv_weight, out_weight):
    levels, lat_cells, lon_cells, width = fields.shape
    rolled = roll_grid(fields, -1)
    windows = to_windows(rolled)
    wincount, tokens_win = (windows.shape[0], windows.shape[1])
    tokens_flat = windows.reshape(-1, width)
    lat_rows = lax.axis_index("lat") * lat_cells + jnp.arange(lat_cells, dtype=jnp.int32)
    group_rows = (lat_rows >= lat_cells * lax.axis_size("lat") - WIN_LAT // 2).astype(jnp.int32)
    group_grid = jnp.broadcast_to(
        group_rows[None, :, None, None], (levels, lat_cells, lon_cells, 1)
    )
    groups = to_windows(group_grid)[..., 0]
    norm_core, norm_back = jax.vjp(normalize, tokens_flat.astype(jnp.float32))
    normed = norm_core.astype(jnp.bfloat16)
    projected = jnp.dot(normed, qkv_weight, preferred_element_type=jnp.float32).astype(jnp.bfloat16)
    mixture, attend_back = jax.vjp(
        lambda values: attend(values, groups), projected.reshape(wincount, tokens_win, 3 * width)
    )
    attended = mixture.reshape(-1, width)
    output_rows = (
        tokens_flat.astype(jnp.float32)
        + jnp.dot(attended, out_weight, preferred_element_type=jnp.float32)
    ).astype(jnp.bfloat16)
    output_field = roll_grid(
        from_windows(
            output_rows.reshape(wincount, tokens_win, width), levels, lat_cells, lon_cells
        ),
        1,
    )
    grad_rows = to_windows(roll_grid(cotangent, -1)).reshape(-1, width)
    out_term = lax.dot_general(
        attended, grad_rows, (((0,), (0,)), ((), ())), preferred_element_type=jnp.float32
    )
    grad_attended = lax.dot_general(
        grad_rows, out_weight, (((1,), (1,)), ((), ())), preferred_element_type=jnp.float32
    ).astype(jnp.bfloat16)
    grad_projected = attend_back(grad_attended.reshape(wincount, tokens_win, width))[0].reshape(
        -1, 3 * width
    )
    qkv_term = lax.dot_general(
        normed, grad_projected, (((0,), (0,)), ((), ())), preferred_element_type=jnp.float32
    )
    grad_normed = lax.dot_general(
        grad_projected, qkv_weight, (((1,), (1,)), ((), ())), preferred_element_type=jnp.float32
    )
    grad_centred = norm_back(grad_normed)[0]
    grad_tokens = (grad_rows.astype(jnp.float32) + grad_centred).astype(jnp.bfloat16)
    field_grad = roll_grid(
        from_windows(
            grad_tokens.reshape(wincount, tokens_win, width), levels, lat_cells, lon_cells
        ),
        1,
    )
    qkv_grad, out_grad = (
        lax.psum_scatter(qkv_term, ("lon", "lat"), scatter_dimension=0, tiled=True),
        lax.psum_scatter(out_term, ("lon", "lat"), scatter_dimension=0, tiled=True),
    )
    return (output_field, field_grad, qkv_grad, out_grad)


def solution(mesh):
    placed = (P(None, "lat", "lon", None), P(None, "lat", "lon", None), P(), P())
    return jax.shard_map(
        shards,
        mesh=mesh,
        in_specs=placed,
        out_specs=(
            P(None, "lat", "lon", None),
            P(None, "lat", "lon", None),
            P(("lon", "lat"), None),
            P(("lon", "lat"), None),
        ),
        check_vma=False,
    )
```

profile of v0, /device:TPU:0, one launch (start us, length us, event | category | flops | bytes accessed | tf_op | source)
XLA Modules:
  0.0 408.3 jit_solution(15153452738002385448)
XLA Ops:
  8.3 5.1 %collective-permute-start.4 = (bf16[2,3,24,512]{3,2,1,0:T(8,128)(2,1)S(1)}, bf16[2,3,24,512]{3,2,1,0:T(8,128)(2,1)S(1)}, u32[]{:S(2)}, u32[]{:S(2)}) collective-permute-start(bf16[2,3,24,512]{3,2,1,0:T(8,128)(2,1)S(1)} %slice.69), channel_id=1, source_target_pairs={{0,3},{1,0},{2,1},{3,2},{4,7},{5,4},{6,5},{7,6},{8,11},{9,8},{10,9... | collective-permute-start | bytes 442376 | tf_op jit(solution)/shard_map/ppermute | solution.py:13
  36.6 3.9 copy.71
  44.5 3.9 reshape.155
  57.4 3.8 reshape.149
  61.1 3.7 convolution_convert_fusion
  66.7 3.6 copy.79
  70.2 3.5 copy.78
  76.8 12.4 %fusion.5 = (f32[8,16,144]{2,1,0:T(8,128)S(1)}, f32[8,16,144,144]{2,3,1,0:T(8,128)}) fusion(pred[8,144,144]{1,2,0:T(8,128)(4,1)S(1)} %copy-done.8, bf16[8,144,16,32]{1,3,2,0:T(8,128)(2,1)} %bitcast.60, bf16[8,144,16,32]{1,3,2,0:T(8,128)(2,1)} %bitcast.58), kind=kOutput, calls=%fused_computation.12 | convolution fusion | flops 177813504 | bytes 13215744 | tf_op jit(solution)/shard_map/jvp(wqhe,wkhe->whqk)/dot_general | solution.py:30
  89.2 11.7 %fusion.16 = f32[8,16,144]{2,1,0:T(8,128)S(1)} fusion(f32[8,16,144]{2,1,0:T(8,128)S(1)} %get-tuple-element.29, f32[8,16,144,144]{2,3,1,0:T(8,128)} %get-tuple-element.30, pred[8,144,144]{1,2,0:T(8,128)(4,1)S(1)} %copy-done.8), kind=kLoop, calls=%fused_computation.25 | loop fusion | flops 10598400 | bytes 10930176 | tf_op jit(solution)/shard_map/jvp()/reduce_sum | solution.py:37
  101.0 21.3 %convert_reduce_fusion = (f32[8,16,144]{2,1,0:T(8,128)}, pred[8,16,144,144]{2,3,1,0:T(8,128)(4,1)}, f32[8,16,144]{2,1,0:T(8,128)S(1)}, bf16[8,16,144,144]{2,3,1,0:T(8,128)(2,1)}) fusion(f32[8,16,144]{2,1,0:T(8,128)S(1)} %get-tuple-element.29, f32[8,16,144,144]{2,3,1,0:T(8,128)} %get-tuple-element.30, pred[8,144,144]{1,2,0:T(8,128)(4,1)S(1)} %copy-done.8, ...), kind=kOutput, calls=%fused_computation.7 | convolution fusion | flops 199028736 | bytes 21399552 | tf_op jit(solution)/shard_map/transpose(jvp(whqk,wkhe->wqhe))/dot_general | solution.py:38
  122.3 21.1 %fusion.33 = (f32[8,16,144]{2,1,0:T(8,128)}, f32[8,16,144,144]{2,3,1,0:T(8,128)}, bf16[8,16,144,144]{2,3,1,0:T(8,128)(2,1)S(1)}) fusion(f32[8,16,144]{2,1,0:T(8,128)S(1)} %get-tuple-element.29, f32[8,16,144,144]{2,3,1,0:T(8,128)} %get-tuple-element.30, pred[8,144,144]{1,2,0:T(8,128)(4,1)S(1)} %copy-done.8, f32[8,16,144]{2,1,0:T(8,128)S(1)} %neg.12, ...), kind=kLoop, calls=%fused_computation.71 | loop fusion | flops 26523648 | bytes 32311296 | tf_op jit(solution)/shard_map/transpose(jvp())/reduce_sum | solution.py:36
  149.9 3.9 convert_element_type.104
  158.4 12.5 %fusion.18 = bf16[8,16,144,32]{2,3,1,0:T(8,128)(2,1)} fusion(bf16[8,144,16,32]{1,3,2,0:T(8,128)(2,1)} %bitcast.61, f32[8,16,144,144]{2,3,1,0:T(8,128)} %get-tuple-element.19, pred[8,16,144,144]{2,3,1,0:T(8,128)(4,1)} %get-tuple-element.21, f32[8,16,144]{2,1,0:T(8,128)S(1)} %negate_divide_fusion, pred[8,144,144]{1,2,0:T(8,128)(4,1)S(1)} %copy-done.8), kind=kOutput, calls=%fused_computation.37 | convolution fusion | flops 181075968 | bytes 15869952 | tf_op jit(solution)/shard_map/transpose(jvp(wqhe,wkhe->whqk))/dot_general | solution.py:30
  170.9 11.2 %fusion.19 = bf16[8,16,144,32]{2,3,1,0:T(8,128)(2,1)} fusion(bf16[8,144,16,32]{1,3,2,0:T(8,128)(2,1)S(1)} %bitcast.59, f32[8,16,144,144]{2,3,1,0:T(8,128)} %get-tuple-element.19, pred[8,16,144,144]{2,3,1,0:T(8,128)(4,1)} %get-tuple-element.21, f32[8,16,144]{2,1,0:T(8,128)S(1)} %negate_divide_fusion, pred[8,144,144]{1,2,0:T(8,128)(4,1)S(1)} %copy-done.8), kind=kOutput, calls=%fused_computation.38 | convolution fusion | flops 181075968 | bytes 15869952 | tf_op jit(solution)/shard_map/transpose(jvp(wqhe,wkhe->whqk))/dot_general | solution.py:30
  190.1 3.7 copy.93
  193.8 8.7 %convolution_convert_fusion.3 = bf16[8,16,32,144]{3,2,1,0:T(8,128)(2,1)} fusion(bf16[8,16,144,144]{2,3,1,0:T(8,128)(2,1)} %copy-done.1, bf16[8,16,32,144]{3,0,2,1:T(8,128)(2,1)} %bitcast.63), kind=kOutput, calls=%fused_computation.39 | convolution fusion | flops 170459136 | bytes 7667712 | tf_op jit(solution)/shard_map/transpose(jvp(whqk,wkhe->wqhe))/dot_general | solution.py:38
  202.5 3.6 copy.88
  209.8 3.9 fusion.37
  223.6 4.2 %multiply_reduce_fusion = (f32[1152]{0:T(1024)S(1)}, f32[1152,512]{1,0:T(8,128)S(1)}) fusion(f32[1152,512]{1,0:T(8,128)S(1)} %copy-done.2, f32[1152]{0:T(1024)S(1)} %div.46, bf16[1152,1536]{1,0:T(8,128)(2,1)} %bitcast.73, bf16[512,1536]{1,0:T(8,128)(2,1)S(1)} %copy-done), kind=kOutput, calls=%fused_computation.33 | convolution fusion | flops 1813707648 | bytes 9839616 | tf_op jit(solution)/shard_map/dot_general | solution.py:121
  228.6 4.4 %collective-permute-done.2 = bf16[2,3,24,512]{3,0,2,1:T(2,128)(2,1)S(1)} collective-permute-done((bf16[2,3,24,512]{3,0,2,1:T(2,128)(2,1)S(1)}, bf16[2,3,24,512]{3,0,2,1:T(2,128)(2,1)S(1)}, u32[]{:S(2)}, u32[]{:S(2)}) %collective-permute-start.2) | collective-permute-done | bytes 147488 | tf_op jit(solution)/shard_map/ppermute | solution.py:13
  241.7 7.2 %collective-permute-done.6 = bf16[2,3,24,512]{3,0,2,1:T(2,128)(2,1)S(1)} collective-permute-done((bf16[2,3,24,512]{3,0,2,1:T(2,128)(2,1)S(1)}, bf16[2,3,24,512]{3,0,2,1:T(2,128)(2,1)S(1)}, u32[]{:S(2)}, u32[]{:S(2)}) %collective-permute-start.6) | collective-permute-done | bytes 147488 | tf_op jit(solution)/shard_map/ppermute | solution.py:13
  252.3 4.4 %collective-permute-done.7 = bf16[2,24,6,512]{3,0,2,1:T(2,128)(2,1)S(1)} collective-permute-done((bf16[2,24,6,512]{3,0,2,1:T(2,128)(2,1)S(1)}, bf16[2,24,6,512]{3,0,2,1:T(2,128)(2,1)S(1)}, u32[]{:S(2)}, u32[]{:S(2)}) %collective-permute-start.7) | collective-permute-done | bytes 294944 | tf_op jit(solution)/shard_map/ppermute | solution.py:13
  259.6 35.7 %reduce-scatter.5.cloned.1.call-done = f32[16,512]{1,0:T(8,128)} async-done(((f32[512,512]{1,0:T(8,128)}), f32[16,512]{1,0:T(8,128)}) %reduce-scatter.5.cloned.1.call-update) | async-done | bytes 32784 | tf_op jit(solution)/shard_map/reduce_scatter | solution.py:134
  295.3 105.7 %reduce-scatter.3.cloned.1.call-done = f32[16,1536]{1,0:T(8,128)} async-done(((f32[512,1536]{1,0:T(8,128)}), f32[16,1536]{1,0:T(8,128)}) %reduce-scatter.3.cloned.1.call-update) | async-done | bytes 98320 | tf_op jit(solution)/shard_map/reduce_scatter | solution.py:133
  (109 shorter events, 90.4 us)
Async XLA Ops:
  7.2 54.0 %copy-start = (bf16[512,1536]{1,0:T(8,128)(2,1)S(1)}, bf16[512,1536]{1,0:T(8,128)(2,1)}, u32[]{:S(2)}) copy-start(bf16[512,1536]{1,0:T(8,128)(2,1)} %param.6) | copy-start | bytes 4718596
  7.2 10.1 %copy-start.10 = (bf16[2,24,24,512]{3,2,1,0:T(8,128)(2,1)S(1)}, bf16[2,24,24,512]{3,2,1,0:T(8,128)(2,1)}, u32[]{:S(2)}) copy-start(bf16[2,24,24,512]{3,2,1,0:T(8,128)(2,1)} %param.5) | copy-start | bytes 3538948
  7.2 288.1 %reduce-scatter.5.cloned.1.call-start = ((), (), s32[]{:S(2)}) async-start(), calls=%async_computation.3 | async-start | bytes 1081344 | tf_op jit(solution)/shard_map/reduce_scatter | solution.py:134
  8.3 12.5 %collective-permute-start.4 = (bf16[2,3,24,512]{3,2,1,0:T(8,128)(2,1)S(1)}, bf16[2,3,24,512]{3,2,1,0:T(8,128)(2,1)S(1)}, u32[]{:S(2)}, u32[]{:S(2)}) collective-permute-start(bf16[2,3,24,512]{3,2,1,0:T(8,128)(2,1)S(1)} %slice.69), channel_id=1, source_target_pairs={{0,3},{1,0},{2,1},{3,2},{4,7},{5,4},{6,5},{7,6},{8,11},{9,8},{10,9... | collective-permute-start | bytes 442376 | tf_op jit(solution)/shard_map/ppermute | solution.py:13
  14.3 5.4 %collective-permute-start = (bf16[2,3,24,512]{3,2,1,0:T(8,128)(2,1)S(1)}, bf16[2,3,24,512]{3,2,1,0:T(8,128)(2,1)S(1)}, u32[]{:S(2)}, u32[]{:S(2)}) collective-permute-start(bf16[2,3,24,512]{3,2,1,0:T(8,128)(2,1)S(1)} %slice.58), channel_id=1, source_target_pairs={{0,3},{1,0},{2,1},{3,2},{4,7},{5,4},{6,5},{7,6},{8,11},{9,8},{10,9... | collective-permute-start | bytes 442376 | tf_op jit(solution)/shard_map/ppermute | solution.py:13
  19.7 6.3 %collective-permute-start.1 = (bf16[2,24,6,512]{3,2,1,0:T(8,128)(2,1)S(1)}, bf16[2,24,6,512]{3,2,1,0:T(8,128)(2,1)S(1)}, u32[]{:S(2)}, u32[]{:S(2)}) collective-permute-start(bf16[2,24,6,512]{3,2,1,0:T(8,128)(2,1)S(1)} %pad_maximum_fusion.4), channel_id=1, source_target_pairs={{0,28},{4,0},{8,4},{12,8},{16,12},{20,16},{24,20},{28,24},{1,29},{... | collective-permute-start | bytes 884744 | tf_op jit(solution)/shard_map/ppermute | solution.py:13
  21.6 26.9 %collective-permute-start.5 = (bf16[2,24,6,512]{3,2,1,0:T(8,128)(2,1)}, bf16[2,24,6,512]{3,2,1,0:T(8,128)(2,1)}, u32[]{:S(2)}, u32[]{:S(2)}) collective-permute-start(bf16[2,24,6,512]{3,2,1,0:T(8,128)(2,1)} %pad_maximum_fusion.3), channel_id=1, source_target_pairs={{0,28},{4,0},{8,4},{12,8},{16,12},{20,16},{24,20},{28,24},{1,29},{... | collective-permute-start | bytes 884744 | tf_op jit(solution)/shard_map/ppermute | solution.py:13
  55.7 5.5 %copy-start.14 = (f32[1152]{0:T(1024)S(1)}, f32[1152]{0:T(1024)}, u32[]{:S(2)}) copy-start(f32[1152]{0:T(1024)} %rsqrt.13) | copy-start | bytes 13828
  73.7 3.0 copy-start.8
  122.3 21.1 %copy-start.3 = (bf16[8,144,512]{1,2,0:T(8,128)(2,1)S(1)}, bf16[8,144,512]{1,2,0:T(8,128)(2,1)}, u32[]{:S(2)}) copy-start(bf16[8,144,512]{1,2,0:T(8,128)(2,1)} %copy.77) | copy-start | bytes 3538948
  143.4 3.7 copy-start.1
  153.8 3.5 copy-start.5
  157.4 243.7 %reduce-scatter.3.cloned.1.call-start = ((), (), s32[]{:S(2)}) async-start(), calls=%async_computation.2 | async-start | bytes 3244032 | tf_op jit(solution)/shard_map/reduce_scatter | solution.py:133
  158.4 12.5 %copy-start.4 = (bf16[8,144,512]{1,2,0:T(8,128)(2,1)S(1)}, bf16[8,144,512]{1,2,0:T(8,128)(2,1)}, u32[]{:S(2)}) copy-start(bf16[8,144,512]{1,2,0:T(8,128)(2,1)} %copy.79) | copy-start | bytes 3538948
  170.9 11.2 %copy-start.13 = (f32[4,2,2,6,12]{4,0,3,2,1:T(4,128)S(1)}, f32[4,2,2,6,12]{4,0,3,2,1:T(4,128)}, u32[]{:S(2)}) copy-start(f32[4,2,2,6,12]{4,0,3,2,1:T(4,128)} %get-tuple-element.27) | copy-start | bytes 13828
  206.1 3.6 copy-start.11
  208.0 1.7 copy-start.9
  213.7 1.4 copy-start.12
  221.0 2.6 copy-start.2
  223.3 9.7 %collective-permute-start.2 = (bf16[2,3,24,512]{3,0,2,1:T(2,128)(2,1)S(1)}, bf16[2,3,24,512]{3,0,2,1:T(2,128)(2,1)S(1)}, u32[]{:S(2)}, u32[]{:S(2)}) collective-permute-start(bf16[2,3,24,512]{3,0,2,1:T(2,128)(2,1)S(1)} %slice.81), channel_id=1, source_target_pairs={{0,1},{1,2},{2,3},{3,0},{4,5},{5,6},{6,7},{7,4},{8,9},{9,10},{10,1... | collective-permute-start | bytes 442376 | tf_op jit(solution)/shard_map/ppermute | solution.py:13
  227.8 5.7 %copy-start.7 = (bf16[1152,512]{1,0:T(8,128)(2,1)S(1)}, bf16[1152,512]{1,0:T(8,128)(2,1)}, u32[]{:S(2)}) copy-start(bf16[1152,512]{1,0:T(8,128)(2,1)} %reshape_reshape.11) | copy-start | bytes 3538948
  233.3 16.1 %collective-permute-start.3 = (bf16[2,24,6,512]{3,0,2,1:T(2,128)(2,1)S(1)}, bf16[2,24,6,512]{3,0,2,1:T(2,128)(2,1)S(1)}, u32[]{:S(2)}, u32[]{:S(2)}) collective-permute-start(bf16[2,24,6,512]{3,0,2,1:T(2,128)(2,1)S(1)} %pad_maximum_fusion.6), channel_id=1, source_target_pairs={{0,4},{4,8},{8,12},{12,16},{16,20},{20,24},{24,28},{28,0},{1,5},{5... | collective-permute-start | bytes 884744 | tf_op jit(solution)/shard_map/ppermute | solution.py:13
  240.8 8.2 %collective-permute-start.6 = (bf16[2,3,24,512]{3,0,2,1:T(2,128)(2,1)S(1)}, bf16[2,3,24,512]{3,0,2,1:T(2,128)(2,1)S(1)}, u32[]{:S(2)}, u32[]{:S(2)}) collective-permute-start(bf16[2,3,24,512]{3,0,2,1:T(2,128)(2,1)S(1)} %slice.85), channel_id=1, source_target_pairs={{0,1},{1,2},{2,3},{3,0},{4,5},{5,6},{6,7},{7,4},{8,9},{9,10},{10,1... | collective-permute-start | bytes 442376 | tf_op jit(solution)/shard_map/ppermute | solution.py:13
  249.3 7.4 %collective-permute-start.7 = (bf16[2,24,6,512]{3,0,2,1:T(2,128)(2,1)S(1)}, bf16[2,24,6,512]{3,0,2,1:T(2,128)(2,1)S(1)}, u32[]{:S(2)}, u32[]{:S(2)}) collective-permute-start(bf16[2,24,6,512]{3,0,2,1:T(2,128)(2,1)S(1)} %pad_maximum_fusion.5), channel_id=1, source_target_pairs={{0,4},{4,8},{8,12},{12,16},{16,20},{20,24},{24,28},{28,0},{1,5},{5... | collective-permute-start | bytes 884744 | tf_op jit(solution)/shard_map/ppermute | solution.py:13
  (1 other events, 1.3 us)
Sparse Core Ops, SparseCore 0:
  157.5 137.7 reduce-scatter.4
  302.2 98.8 reduce-scatter.2
where the time goes:
time: 414 us; the launch traced here: 408 us
  waiting for transfers between devices  162 us (39%)
  matrix products  89.4 us (22%)
  local copies, waits for them, and re-layouts  76.6 us (19%)
  other arithmetic  56.3 us (14%)
  between operations  14.9 us (4%)
  starting transfers between devices  8.93 us (2%)
    reduce_scatter x1, waiting for transfers between devices, shards(): lax.psum_scatter(qkv_term, ('lon', 'lat'), scatter_dimension=0, tiled=True)  106 us
    dot_general x3, matrix products, attend(): jnp.einsum('wqhe,wkhe->whqk', queries, keyset, preferred_element_type=jnp...  36.1 us
    reduce_scatter x1, waiting for transfers between devices, shards(): lax.psum_scatter(out_term, ('lon', 'lat'), scatter_dimension=0, tiled=True)  35.7 us
    dot_general x3, matrix products, attend(): jnp.einsum('whqk,wkhe->wqhe', soft_weights, valueset, preferred_element_t...  31.3 us
    reduce_sum x1, other arithmetic, attend(): raised = jnp.exp(scores - highest)  21.1 us
    ppermute x8, waiting for transfers between devices, from_behind(): lax.ppermute(x, axis, [(i, (i + by) % length) for i in range(length)])  20.7 us
    reduce_sum x1, other arithmetic, attend(): jnp.sum(raised, axis=-1, keepdims=True)  11.7 us
    convert_element_type x3, local copies, waits for them, and re-layouts, shards(): tokens_flat.astype(jnp.float32)  11 us
  transfers between devices with their start and end apart: 10, of which 7 were waited for; matrix products, arithmetic and copies ran while one was open for 27% of the time, Pallas kernels for 0%

commit v1 on v0

v1 whole, which is shorter than its diff:
```python
import functools

import jax
import jax.numpy as jnp
from jax import lax
from jax.experimental import pallas as pl
from jax.experimental.pallas import tpu as pltpu
from jax.sharding import PartitionSpec as P

HEADS = 16
WIN_LAT = 6
WIN_LON = 12
TOKENS = 144
MAIN = 128
TAIL = TOKENS - MAIN
GROUP = 8
F32 = jnp.float32
BF16 = jnp.bfloat16
VMEM_LIMIT = 36 * 1024 * 1024


def nn(a, b):
    return lax.dot_general(a, b, (((1,), (0,)), ((), ())), preferred_element_type=F32)


def nt(a, b):
    return lax.dot_general(a, b, (((1,), (1,)), ((), ())), preferred_element_type=F32)


def sublane(shape):
    return lax.broadcasted_iota(jnp.int32, shape, len(shape) - 2)


def inner_lanes(shape):
    sub = sublane(shape)
    return (sub >= 2) & (sub < 6)


def first_window(a, b, c):
    width = b.shape[-1]
    edge = jnp.where(sublane(a.shape) >= 6, a, c)
    inner = inner_lanes((6,) + a.shape[1:])
    mixed = jnp.where(inner, jnp.roll(edge[6:], 4, axis=1), edge[:6])
    return jnp.concatenate([b.reshape(96, width), mixed.reshape(48, width)], axis=0)


def second_window(a, c):
    width = a.shape[-1]
    late = jnp.where(sublane(a.shape) < 6, a, c)
    inner = inner_lanes((6,) + a.shape[1:])
    mixed = jnp.where(inner, c[:6], jnp.roll(c[6:], 4, axis=1))
    return jnp.concatenate([late.reshape(96, width), mixed.reshape(48, width)], axis=0)


def windows_to_band(w0, w1):
    width = w0.shape[-1]
    b = w0[:96].reshape(12, 8, width)
    late = w1[:96].reshape(12, 8, width)
    first = w0[96:].reshape(6, 8, width)
    second = w1[96:].reshape(6, 8, width)
    edge = jnp.concatenate([first, jnp.roll(first, 4, axis=1)], axis=0)
    mid = jnp.concatenate([second, jnp.roll(second, 4, axis=1)], axis=0)
    sub = sublane(b.shape)
    a = jnp.where(sub < 6, late, edge)
    c = jnp.where(sub < 2, edge, jnp.where(sub < 6, mid, late))
    return a, b, c


def statistics(x):
    center = jnp.mean(x, axis=-1, keepdims=True)
    centred = x - center
    spread = jnp.mean(centred * centred, axis=-1, keepdims=True)
    return centred, lax.rsqrt(spread + 1e-05)


class Copies:
    def __init__(self, sems):
        self.sems = sems
        self.used = 0

    def start(self, source, target):
        copy = pltpu.make_async_copy(source, target, self.sems.at[self.used])
        self.used += 1
        copy.start()
        return copy


def pack_edges(sets):
    last = sets[3].astype(F32)
    whole = sublane(last.shape) < 6
    return [
        jnp.where(whole, sets[k].astype(F32), jnp.roll(last, 6 - 2 * k, axis=1)).astype(BF16)
        for k in range(3)
    ]


def edge_rows(lon_ref, arr, level, start, size):
    parts = [lon_ref[k, start : start + size].astype(F32) for k in range(3)]
    if 2 * arr + level < 3:
        return parts[2 * arr + level]
    sub = sublane(parts[0].shape)
    late = jnp.where(sub < 4, jnp.roll(parts[1], 4, axis=1), jnp.roll(parts[2], 6, axis=1))
    return jnp.where(sub < 2, jnp.roll(parts[0], 2, axis=1), late)


def pack_kernel(f_hbm, c_hbm, lat_ref, lon_ref, cor_ref, edge_ref, sems):
    copies = Copies(sems)
    waits = []
    for arr, hbm in enumerate((f_hbm, c_hbm)):
        waits.append(copies.start(hbm.at[:, 3:, :16], edge_ref.at[arr]))
        waits.append(copies.start(hbm.at[:, :3], lat_ref.at[arr]))
    for wait in waits:
        wait.wait()
    cor_ref[...] = lat_ref[:, :, :, :8]
    sets = [edge_ref[k // 2, k % 2, :, :8] for k in range(4)]
    for k, packed in enumerate(pack_edges(sets)):
        lon_ref[k] = packed


def own_band(src, start):
    planes = [src[level, start : start + WIN_LAT].astype(F32) for level in range(2)]
    x = jnp.concatenate(planes, axis=0)
    return x[:, 0:8], x[:, 8:16], x[:, 16:24]


def with_neighbours(src, lat_ref, lon_ref, cor_ref, arr, band):
    start = 3 + band * WIN_LAT
    rows = src.shape[1]
    planes, edges = [], []
    for level in range(2):
        if start + WIN_LAT <= rows:
            planes.append(src[level, start : start + WIN_LAT])
            edges.append(edge_rows(lon_ref, arr, level, start - 3, WIN_LAT))
        else:
            planes.extend([src[level, start:], lat_ref[arr, level]])
            edges.extend([edge_rows(lon_ref, arr, level, start - 3, 3), cor_ref[arr, level]])
    x = jnp.concatenate([p.astype(F32) for p in planes], axis=0)
    edge = jnp.concatenate([e.astype(F32) for e in edges], axis=0)
    a = jnp.where(sublane(edge.shape) < 6, edge, x[:, 0:8])
    return a, x[:, 8:16], x[:, 16:24]


def store_window(arr, values, place, x_ref, n_ref, g_ref):
    if arr == 0:
        x_ref[place] = values.astype(BF16)
        centred, scale = statistics(values)
        n_ref[place] = (centred * scale).astype(BF16)
    else:
        g_ref[place] = values.astype(BF16)


def extend(x):
    return jnp.concatenate([x[:MAIN]] + [x[MAIN:]] * GROUP, axis=0)


def tail_mask():
    rows = lax.broadcasted_iota(jnp.int32, (256, 128), 0) // 32
    lanes = lax.broadcasted_iota(jnp.int32, (256, 128), 1) // TAIL
    return rows == lanes


def head_tile(block, head):
    parts = []
    if head > 0:
        parts.append(jnp.zeros((32 * head, 128), block.dtype))
    parts.append(block)
    if head < GROUP - 1:
        parts.append(jnp.zeros((32 * (GROUP - 1 - head), 128), block.dtype))
    return jnp.concatenate(parts, axis=0)


def window_attention(normed, grads, natural_kv, wt, wo, bias, fold, att_ref, dp_ref):
    head_size = 32
    scale = head_size ** (-0.5)
    factor = scale * 1.4426950408889634
    mask = tail_mask()
    groups = range(2)
    turned = nt(wt, extend(normed)).astype(BF16)
    turned_grads = nt(wo, extend(grads))
    turned_kv = natural_kv.T
    keys = [natural_kv[:, 256 * g : 256 * g + 256] for g in groups]
    values = [natural_kv[:, 512 + 256 * g : 768 + 256 * g] for g in groups]
    kt = [turned_kv[256 * g : 256 * g + 256] for g in groups]
    vt = [turned_kv[512 + 256 * g : 768 + 256 * g] for g in groups]
    dot = [turned_grads[256 * g : 256 * g + 256] for g in groups]

    def tiles_of(main, tail):
        tiles = []
        for j in range(GROUP // 2):
            tiles.append(
                jnp.concatenate(
                    [head_tile(main[32 * h : 32 * h + 32], h) for h in (2 * j, 2 * j + 1)], axis=1
                )
            )
        return tiles + [tail]

    q_tiles = []
    for g in groups:
        part = turned[256 * g : 256 * g + 256]
        q_tiles.append(tiles_of(part[:, :128], jnp.where(mask, part[:, 128:], jnp.zeros((), BF16))))
    yield
    order = [(j, g) for j in range(GROUP // 2 + 1) for g in groups]
    ahead = 2

    def channels(rows, tile, j):
        if j == GROUP // 2:
            return nn(rows, tile)
        first = 128 * (j // 2)
        return nn(rows[:, first : first + 128], tile[first : first + 128])

    def score(j, g):
        scores = channels(keys[g], q_tiles[g][j], j)
        if bias is None:
            return scores
        part = bias[:, :128] if j < 4 else bias[:, 128:]
        return scores + (jnp.concatenate([part, part], axis=1) if j < 4 else part)

    soft = [[], []]
    inverse = [[], []]
    mixed = [[], []]
    waiting = [score(*at) for at in order[:ahead]]
    for i, (j, g) in enumerate(order):
        if i + ahead < len(order):
            waiting.append(score(*order[i + ahead]))
        scores = waiting[i]
        raised = jnp.exp2((scores - jnp.max(scores, axis=0, keepdims=True)) * factor)
        inv = 1.0 / jnp.sum(raised, axis=0, keepdims=True)
        held = raised.astype(BF16)
        soft[g].append(held)
        inverse[g].append(inv)
        if j < 4:
            out = nn(vt[g][64 * j : 64 * j + 64], held)
            mixed[g].append(out[:32, :128] * inv[:, :128])
            mixed[g].append(out[32:, 128:] * inv[:, 128:])
        else:
            out = nn(vt[g], held)
            mixed[g].append(jnp.where(mask, out * inv, 0.0))
        yield
    do_tiles = [None, None]
    deltas = [None, None]
    for g in groups:
        scaled, sums = [], []
        for h in range(GROUP):
            inv = inverse[g][h // 2][:, 128 * (h % 2) : 128 * (h % 2) + 128]
            scaled.append((dot[g][32 * h : 32 * h + 32, :128] * inv).astype(BF16))
            sums.append(jnp.sum(scaled[h].astype(F32) * mixed[g][h], axis=0, keepdims=True))
        tail = jnp.where(mask, dot[g][:, 128:] * inverse[g][4], 0.0).astype(BF16)
        deltas[g] = [jnp.concatenate(sums[2 * j : 2 * j + 2], axis=1) for j in range(GROUP // 2)]
        deltas[g].append(jnp.sum(tail.astype(F32) * mixed[g][GROUP], axis=0, keepdims=True))
        do_tiles[g] = tiles_of(jnp.concatenate(scaled, axis=0), tail)
        yield
    slopes = [[], []]
    dq = [[], []]
    waiting = [channels(values[g], do_tiles[g][j], j) for j, g in order[:ahead]]
    for i, (j, g) in enumerate(order):
        if i + ahead < len(order):
            k, f = order[i + ahead]
            waiting.append(channels(values[f], do_tiles[f][k], k))
        slope = (soft[g][j].astype(F32) * (waiting[i] - deltas[g][j])).astype(BF16)
        slopes[g].append(slope)
        if j < 4:
            out = nn(kt[g][64 * j : 64 * j + 64], slope) * scale
            dq[g].append(out[:32, :128])
            dq[g].append(out[32:, 128:])
        else:
            out = nn(kt[g], slope) * scale
            dq[g].append(jnp.where(mask, out, 0.0))
        yield
    def by_keys(rows, tiles):
        halves = []
        for i in range(2):
            part = slice(128 * i, 128 * i + 128)
            pair = (2 * i, 2 * i + 1)
            halves.append(
                nt(
                    jnp.concatenate([rows[j] for j in pair], axis=1),
                    jnp.concatenate([tiles[j][part] for j in pair], axis=1),
                )
            )
        return jnp.concatenate(halves, axis=1) + nt(rows[GROUP // 2], tiles[GROUP // 2])

    def natural(blocks):
        main = jnp.concatenate(blocks[:GROUP], axis=0)
        tail = nt(fold, blocks[GROUP].astype(BF16))
        return jnp.concatenate([main.T, tail], axis=0)

    for g in groups:
        span = slice(256 * g, 256 * g + 256)
        att_ref[:, span] = natural(mixed[g]).astype(BF16)
        yield
        dv = by_keys(soft[g], do_tiles[g])
        dp_ref[:, 1024 + 256 * g : 1280 + 256 * g] = dv.astype(BF16)
        yield
        dk = by_keys(slopes[g], q_tiles[g]) * scale
        dp_ref[:, 512 + 256 * g : 768 + 256 * g] = dk.astype(BF16)
        yield
        dp_ref[:, span] = natural(dq[g]).astype(BF16)
        yield


FORWARD = 12


def in_turns(windows):
    waiting, active, done = list(windows), [], {}
    while waiting or active:
        if waiting and (not active or (len(active) < 3 and done[active[-1][0]] >= FORWARD)):
            number = len(windows) - len(waiting)
            active.append((number, waiting.pop(0)))
            done[number] = 0
        for item in list(active):
            try:
                next(item[1])
                done[item[0]] += 1
            except StopIteration:
                active.remove(item)


def fill_bias(bias_ref, last):
    def row_of(token):
        return jnp.where(token < 96, (token // 8) % 6, (token - 96) // 8) >= 3

    keys = row_of(lax.broadcasted_iota(jnp.int32, (TOKENS, 256), 0))
    lane = lax.broadcasted_iota(jnp.int32, (TOKENS, 256), 1)
    queries = row_of(jnp.where(lane < MAIN, lane, MAIN + lane % TAIL))
    bias_ref[...] = jnp.where((keys != queries) & (last == 1), -1e10, 0.0)


def split_rows(total_ref, core, mine_ref, send_ref):
    count, rows = mine_ref.shape[0], mine_ref.shape[1]
    for i in range(count):
        mine_ref[i] = total_ref[pl.ds((2 * i + core) * rows, rows)]
        send_ref[i] = total_ref[pl.ds((2 * i + 1 - core) * rows, rows)]


def fold_matrix():
    lanes = lax.broadcasted_iota(jnp.int32, (TAIL, 128), 1) % TAIL
    return (lanes == lax.broadcasted_iota(jnp.int32, (TAIL, 128), 0)).astype(BF16)


def flat(ref):
    return ref[...].reshape(-1, ref.shape[-1])


def back_of_windows(x_ref, g_ref, att_ref, dp_ref, w, wo):
    mixture = nn(flat(att_ref), wo)
    grads = nt(flat(dp_ref), w)
    pairs = []
    for i in range(x_ref.shape[0]):
        rows = slice(TOKENS * i, TOKENS * i + TOKENS)
        x, grad = x_ref[i].astype(F32), grads[rows]
        centred, scale = statistics(x)
        hat = centred * scale
        back = grad - jnp.mean(grad, axis=-1, keepdims=True)
        back = back - hat * jnp.mean(grad * hat, axis=-1, keepdims=True)
        tokens = g_ref[i].astype(F32) + back * scale
        pairs.append(((x + mixture[rows]).astype(BF16), tokens.astype(BF16)))
    return pairs


def inner_kernel(f_hbm, c_hbm, w_ref, wo_ref, *refs):
    outs, (f_ref, c_ref, x_ref, kv_ref, wt_ref, sems), results = refs[:6], refs[6:12], refs[12:]
    n_ref, g_ref, att_ref, dp_ref, out_ref, grad_ref = results
    copies = Copies(sems)
    count = n_ref.shape[0]
    rows = [pl.ds(3 + band * WIN_LAT, WIN_LAT) for band in range(count)]
    got = [
        [copies.start(hbm.at[:, rows[band]], ref.at[band]) for band in range(count)]
        for hbm, ref in ((f_hbm, f_ref), (c_hbm, c_ref))
    ]

    def front(arr, src):
        for band in range(count):
            got[arr][band].wait()
            store_window(arr, first_window(*own_band(src[band], 0)), band, x_ref, n_ref, g_ref)

    wt_ref[...] = w_ref[:, :512].T
    front(0, f_ref)
    kv_ref[...] = nn(flat(n_ref), w_ref[:, 512:]).astype(BF16).reshape(kv_ref.shape)
    front(1, c_ref)
    sent = [copies.start(results[k], outs[k]) for k in range(2)]
    fold = fold_matrix()

    in_turns(
        [
            window_attention(
                n_ref[i],
                g_ref[i],
                kv_ref[i],
                wt_ref[...],
                wo_ref[...],
                None,
                fold,
                att_ref.at[i],
                dp_ref.at[i],
            )
            for i in range(count)
        ]
    )
    sent += [copies.start(results[k], outs[k]) for k in (2, 3)]
    pairs = back_of_windows(x_ref, g_ref, att_ref, dp_ref, w_ref[...], wo_ref[...])
    for i, (out, grad) in enumerate(pairs):
        out_ref[i] = out
        grad_ref[i] = grad
        sent += [copies.start(results[k].at[i], outs[k].at[i]) for k in (4, 5)]
    for copy in sent:
        copy.wait()


def outer_kernel(where_ref, f_hbm, c_hbm, lat_ref, lon_ref, cor_ref, w_ref, wo_hbm, *refs):
    ins, refs = refs[:4], refs[4:]
    x_ref, g_ref, att_ref, dp_ref, mine_ref, send_ref, f_ref, c_ref = refs[:8]
    held, (wo_ref, n_ref, kv_ref, wt_ref, bias_ref, total_ref, sems) = refs[8:12], refs[12:]
    copies = Copies(sems)
    count = n_ref.shape[0]
    bands = count - 1
    spans = []
    for band in range(bands):
        start = 3 + band * WIN_LAT
        spans.append(pl.ds(start, min(WIN_LAT, f_ref.shape[1] - start)))
    got = [
        [copies.start(hbm.at[:, span], ref.at[:, span]) for span in spans]
        for hbm, ref in ((f_hbm, f_ref), (c_hbm, c_ref))
    ]
    wo_copy = copies.start(wo_hbm, wo_ref)
    terms = [copies.start(*pair) for pair in zip(ins, held)]

    def front(arr, src):
        for band in range(bands):
            got[arr][band].wait()
            a, b, c = with_neighbours(src, lat_ref, lon_ref, cor_ref, arr, band)
            store_window(arr, second_window(a, c), band, x_ref, n_ref, g_ref)
            if band == bands - 1:
                store_window(arr, first_window(a, b, c), band + 1, x_ref, n_ref, g_ref)

    wt_ref[...] = w_ref[:, :512].T
    fill_bias(bias_ref, where_ref[0])
    front(0, f_ref)
    kv_ref[...] = nn(flat(n_ref), w_ref[:, 512:]).astype(BF16).reshape(kv_ref.shape)
    front(1, c_ref)
    fold = fold_matrix()

    wo_copy.wait()
    in_turns(
        [
            window_attention(
                n_ref[i],
                g_ref[i],
                kv_ref[i],
                wt_ref[...],
                wo_ref[...],
                bias_ref[...] if i >= bands - 1 else None,
                fold,
                att_ref.at[i],
                dp_ref.at[i],
            )
            for i in range(count)
        ]
    )
    for copy in terms:
        copy.wait()
    inner_n, inner_g, inner_att, inner_dp = held
    total_ref[:, :1536] = (
        nn(flat(n_ref).T, flat(dp_ref)) + nn(flat(inner_n).T, flat(inner_dp))
    ).astype(BF16)
    total_ref[:, 1536:] = (
        nn(flat(att_ref).T, flat(g_ref)) + nn(flat(inner_att).T, flat(inner_g))
    ).astype(BF16)
    split_rows(total_ref, where_ref[1], mine_ref, send_ref)


def outer_back_kernel(x_ref, g_ref, att_ref, dp_ref, w_ref, wo_ref, *refs):
    outs, (lat_out, lon_out), results, sems = refs[:2], refs[2:4], refs[4:6], refs[6]
    copies = Copies(sems)
    count = x_ref.shape[0]
    bands = count - 1
    sent = []
    pairs = back_of_windows(x_ref, g_ref, att_ref, dp_ref, w_ref[...], wo_ref[...])
    for i, pair in enumerate(pairs):
        for values, ref, hbm in zip(pair, results, outs):
            ref[i] = values
            sent.append(copies.start(ref.at[i], hbm.at[i]))
    sets = []
    for arr, ref in enumerate(results):
        edges = [ref[band, :96].reshape(12, 8, 512) for band in range(bands)]
        for level in range(2):
            first = WIN_LAT * level
            rows = [edge[first : first + WIN_LAT] for edge in edges[:-1]]
            sets.append(jnp.concatenate(rows + [edges[-1][first : first + 3]], axis=0))
        a, b, c = windows_to_band(ref[bands].astype(F32), ref[bands - 1].astype(F32))
        planes = jnp.concatenate([a, b, c], axis=1).astype(BF16)
        for level in range(2):
            lat_out[arr, level] = planes[WIN_LAT * level + 3 : WIN_LAT * level + 6]
    for k, packed in enumerate(pack_edges(sets)):
        lon_out[k] = packed
    for copy in sent:
        copy.wait()


def forward_kernel(lat_ref, lon_ref, out_ref):
    rows = lon_ref.shape[1]
    sets = [lat_ref[k // 2, k % 2, :, :8] for k in range(4)]
    for k, packed in enumerate(pack_edges(sets)):
        out_ref[k, :rows] = lon_ref[k]
        out_ref[k, rows:] = packed


def merge_kernel(*refs):
    ins, lat_ref, outs, (left_ref, *refs) = refs[:4], refs[4], refs[5:7], refs[7:]
    held, results, sems = refs[:4], refs[4:6], refs[6]
    copies = Copies(sems)
    got = [copies.start(ins[k], held[k]) for k in range(4)]
    rows = results[0].shape[1]
    bands = rows // WIN_LAT
    sent = []
    for arr, dest in enumerate(results):
        first, second = held[2 * arr], held[2 * arr + 1]
        for level in range(2):
            dest[level, :3] = lat_ref[arr, level]
        got[2 * arr].wait()
        got[2 * arr + 1].wait()
        for band in range(bands):
            w0 = first[band] if band < bands - 1 else second[bands]
            a, b, c = windows_to_band(w0.astype(F32), second[band].astype(F32))
            planes = jnp.concatenate([a, b, c], axis=1).astype(BF16)
            start = 3 + band * WIN_LAT
            size = min(WIN_LAT, rows - start)
            for level in range(2):
                own = slice(level * WIN_LAT, level * WIN_LAT + size)
                dest[level, start : start + size] = planes[own]
        sent.append(copies.start(dest, outs[arr]))
        left_ref[arr] = dest[:, :, :16]
    for copy in sent:
        copy.wait()


def patch_kernel(left_ref, lon_ref, out_hbm, grad_hbm, out_new, grad_new, patch_ref, sems):
    copies = Copies(sems)
    rows = left_ref.shape[2]
    sent = []
    for arr, hbm in enumerate((out_new, grad_new)):
        for level in range(2):
            for start, place, size in ((0, 3, rows - 3), (rows - 3, 0, 3)):
                edge = edge_rows(lon_ref, arr, level, start, size)
                tile = left_ref[arr, level, place : place + size].astype(F32)
                left = jnp.where(sublane(edge.shape) < 6, edge, tile[:, :8])
                tile = jnp.concatenate([left, tile[:, 8:]], axis=1).astype(BF16)
                patch_ref[arr, level, place : place + size] = tile
        sent.append(copies.start(patch_ref.at[arr], hbm.at[:, :, :16]))
    for copy in sent:
        copy.wait()


def pair_kernel(mine_ref, other_ref, out_ref):
    out_ref[...] = (mine_ref[...].astype(F32) + other_ref[...].astype(F32)).astype(BF16)


def halve_kernel(where_ref, mine_ref, other_ref, *refs):
    kept, sent = refs[:2], refs[2:]
    half = kept[0].shape[-1]
    x, y = where_ref[3], where_ref[4]

    def terms(chip, columns):
        return mine_ref[chip, :, columns].astype(F32) + other_ref[chip, :, columns].astype(F32)

    for k in range(2):
        first, second = slice(0, half), slice(half, 2 * half)
        kept[0][k] = terms(2 * k + x, first).astype(BF16)
        sent[0][k] = terms(2 * k + 1 - x, first).astype(BF16)
        kept[1][k] = terms(2 * y + k, second).astype(BF16)
        sent[1][k] = terms(2 * (1 - y) + k, second).astype(BF16)


def quarter_kernel(where_ref, *refs):
    kept, got, keep, send = refs[:2], refs[2:4], refs[4:6], refs[6:8]
    x, y = where_ref[3], where_ref[4]
    for arr, bit in ((0, y), (1, x)):
        keep[arr][...] = kept[arr][bit].astype(F32) + got[arr][bit].astype(F32)
        out = kept[arr][1 - bit].astype(F32) + got[arr][1 - bit].astype(F32)
        send[arr][...] = out.astype(BF16)


def spread(where_ref, total, own_ref, sends, held_ref):
    count, rows = held_ref.shape[0], held_ref.shape[1]
    for i in range(count):
        held_ref[i] = total[rows * i : rows * i + rows]
    me = where_ref[2]
    own_ref[...] = held_ref[me]
    for k, ref in enumerate(sends):
        ref[...] = held_ref[lax.rem(me + 1 + k, count)].astype(BF16)


def pieces_kernel(where_ref, pieces_ref, own_ref, *refs):
    total = pieces_ref[0].astype(F32)
    for i in range(1, pieces_ref.shape[0]):
        total = total + pieces_ref[i].astype(F32)
    spread(where_ref, total, own_ref, refs[:-1], refs[-1])


def halves_kernel(where_ref, *refs):
    keep, got, (own_ref, *refs) = refs[:2], refs[2:4], refs[4:]
    sums = [keep[arr][...] + got[arr][...].astype(F32) for arr in range(2)]
    spread(where_ref, jnp.concatenate(sums, axis=1), own_ref, refs[:-1], refs[-1])


def owner_kernel(own_ref, *refs):
    total = own_ref[...]
    for ref in refs[:-2]:
        total = total + ref[...].astype(F32)
    qkv_ref, out_ref = refs[-2:]
    width = qkv_ref.shape[-1]
    qkv_ref[...] = total[:, :width]
    out_ref[...] = total[:, width:]


def shapes(*items):
    return [jax.ShapeDtypeStruct(shape, dtype) for shape, dtype in items]


VMEM = pl.BlockSpec(memory_space=pltpu.VMEM)
SMEM = pl.BlockSpec(memory_space=pltpu.SMEM)
HBM = pl.BlockSpec(memory_space=pltpu.HBM)


def call(kernel, args, out_shape, micros, scratch=(), scalars=0, ins=VMEM, outs=VMEM, aliases=None):
    moved = sum(a.size * a.dtype.itemsize for a in args)
    out_specs = list(outs) if isinstance(outs, (list, tuple)) else [outs] * len(out_shape)
    out_shape = [
        pltpu.HBM(item.shape, item.dtype) if spec is HBM else item
        for item, spec in zip(out_shape, out_specs)
    ]
    in_specs = list(ins) if isinstance(ins, (list, tuple)) else [ins] * (len(args) - scalars)
    args = [
        pltpu.with_memory_space_constraint(arg, pltpu.HBM) if spec is HBM else arg
        for arg, spec in zip(args, [SMEM] * scalars + in_specs)
    ]
    return pl.pallas_call(
        kernel,
        out_shape=out_shape,
        in_specs=[SMEM] * scalars + in_specs,
        out_specs=out_specs,
        scratch_shapes=list(scratch),
        input_output_aliases=aliases or {},
        compiler_params=pltpu.CompilerParams(vmem_limit_bytes=VMEM_LIMIT),
        cost_estimate=pl.CostEstimate(
            flops=int(micros * 10**9), bytes_accessed=moved, transcendentals=0
        ),
    )(*args)


def room(items):
    return [pltpu.VMEM(item.shape, item.dtype) for item in items]


def shift(x, lon_by, lat_by):
    lons, lats = lax.axis_size("lon"), lax.axis_size("lat")
    pairs = []
    for i in range(lons):
        for j in range(lats):
            to = (i + lon_by) % lons * lats + (j + lat_by) % lats
            pairs.append((i * lats + j, to))
    return lax.ppermute(x, ("lon", "lat"), pairs)


def partner(x, axis, flip):
    return lax.ppermute(x, axis, [(i, i ^ flip) for i in range(lax.axis_size(axis))])


def exchange(pieces, axis, groups=None):
    return lax.all_to_all(pieces, axis, 0, 0, axis_index_groups=groups, tiled=True)


def shards(fields, cotangent, qkv_weight, out_weight):
    levels, lat_cells, lon_cells, width = fields.shape
    lons, lats = lax.axis_size("lon"), lax.axis_size("lat")
    sems = pltpu.SemaphoreType.DMA
    halos = shapes(
        ((2, 2, 3, lon_cells, width), BF16),
        ((3, lat_cells - 3, 8, width), BF16),
        ((2, 2, 3, 8, width), BF16),
    )
    lat_edge, lon_edge, corner = call(
        pack_kernel,
        (fields, cotangent),
        halos,
        1,
        scratch=[pltpu.VMEM((2, 2, lat_cells - 3, 16, width), BF16), sems((4,))],
        ins=HBM,
    )
    lon_edge = shift(lon_edge, -1, 0)
    lat_edge = shift(lat_edge, 0, -1)
    corner = shift(corner, -1, -1)
    row = lax.axis_index("lat")
    lon = lax.axis_index("lon")
    position = jnp.stack(
        [(row == lats - 1).astype(jnp.int32), lon % 2, row, lon // 2 % 2, lon // 4 % 2]
    )
    bands = lat_cells // WIN_LAT

    def windows(count, cols=width):
        return jax.ShapeDtypeStruct((count, TOKENS, cols), BF16)

    def whole(*shape):
        return jax.ShapeDtypeStruct(shape, BF16)

    count = bands - 1
    state = [windows(count)] * 3 + [windows(count, 3 * width)] + [windows(count)] * 2
    band = whole(count, levels, WIN_LAT, lon_cells, width)
    *in_terms, out_in, grad_in = call(
        inner_kernel,
        (fields, cotangent, qkv_weight, out_weight),
        state,
        11,
        scratch=room((band, band, windows(count)))
        + room((windows(count, 2 * width), whole(width, width)))
        + [sems((4 * count + 4,))]
        + room(state),
        ins=[HBM, HBM, VMEM, VMEM],
        outs=HBM,
    )
    count = bands + 1
    rows = width // lons
    terms = whole(lons // 2, rows, 4 * width)
    weights = (qkv_weight, out_weight)
    *outer, mine, send = call(
        outer_kernel,
        (position, fields, cotangent, lat_edge, lon_edge, corner, *weights, *in_terms),
        [windows(count)] * 3 + [windows(count, 3 * width), terms, terms],
        20,
        scratch=room((fields, cotangent, *in_terms, out_weight))
        + room((windows(count), windows(count, 2 * width), whole(width, width)))
        + [pltpu.VMEM((TOKENS, 256), F32), pltpu.VMEM((width, 4 * width), BF16)]
        + [sems((2 * bands + 5,))],
        scalars=1,
        ins=[HBM] * 2 + [VMEM] * 4 + [HBM] * 5,
    )
    received = partner(send, "lon", 1)
    square = lons // 2 == 4
    chips = [[2 * i + core for i in range(lons // 2)] for core in range(2)]
    if square:
        half = whole(2, rows, 2 * width)
        *kept, first, second = call(
            halve_kernel, (position, mine, received), [half] * 4, 1, scalars=1
        )
        first, second, outer[0] = lax.optimization_barrier((first, second, outer[0]))
        parts = [partner(first, "lon", 2), partner(second, "lon", 4)]
    else:
        (total,) = call(pair_kernel, (mine, received), [terms], 1)
        total, outer[0] = lax.optimization_barrier((total, outer[0]))
        parts = [exchange(total, "lon", chips)]
    results = [windows(count)] * 2
    out_out, grad_out, lat_out, lon_out = call(
        outer_back_kernel,
        (*outer, *weights),
        results + halos[:2],
        5,
        scratch=room(results) + [sems((2 * count,))],
        outs=[HBM] * 2 + [VMEM] * 2,
    )
    parts, lon_out = lax.optimization_barrier((parts, lon_out))
    lat_out = shift(lat_out, 0, 1)
    (lon_out,) = call(forward_kernel, (lat_out, lon_out), [whole(3, lat_cells, 8, width)], 1)
    own = width // (lons * lats)
    shares = shapes(((own, 4 * width), F32), *[((own, 4 * width), BF16)] * (lats - 1))
    if square:
        quarter = (rows, 2 * width)
        *kept, first, second = call(
            quarter_kernel,
            (position, *kept, *parts),
            shapes((quarter, F32), (quarter, F32), (quarter, BF16), (quarter, BF16)),
            1,
            scalars=1,
        )
        parts = [partner(first, "lon", 4), partner(second, "lon", 2)]
        parts, _ = lax.optimization_barrier((parts, lon_out))
        parts = (*kept, *parts)
    lon_out = shift(lon_out, 1, 0)
    own, *sends = call(
        halves_kernel if square else pieces_kernel,
        (position, *parts),
        shares,
        1,
        scratch=[pltpu.VMEM((lats, own, 4 * width), F32)],
        scalars=1,
    )
    sends, out_in, grad_in = lax.optimization_barrier((sends, out_in, grad_in))
    got = [shift(piece, 0, 1 + k) for k, piece in enumerate(sends)]
    args = (out_in, out_out, grad_in, grad_out)
    results = shapes((fields.shape, BF16), (fields.shape, BF16))
    left = whole(2, levels, lat_cells, 16, width)
    *results, left = call(
        merge_kernel,
        args + (lat_out,),
        results + [left],
        4,
        scratch=room(args) + room(results) + [sems((6,))],
        ins=[HBM] * 4 + [VMEM],
        outs=[HBM] * 2 + [VMEM],
    )
    output_field, field_grad = call(
        patch_kernel,
        (left, lon_out, *results),
        results,
        2,
        scratch=room((left,)) + [sems((2,))],
        ins=[VMEM] * 2 + [HBM] * 2,
        outs=HBM,
        aliases={2: 0, 3: 1},
    )
    got, output_field, field_grad = lax.optimization_barrier((got, output_field, field_grad))
    qkv_grad, out_grad = call(
        owner_kernel,
        (own, *got),
        shapes(((own.shape[0], 3 * width), F32), ((own.shape[0], width), F32)),
        1,
    )
    return output_field, field_grad, qkv_grad, out_grad


def solution(mesh):
    placed = (P(None, "lat", "lon", None), P(None, "lat", "lon", None), P(), P())
    return jax.shard_map(
        shards,
        mesh=mesh,
        in_specs=placed,
        out_specs=(
            P(None, "lat", "lon", None),
            P(None, "lat", "lon", None),
            P(("lon", "lat"), None),
            P(("lon", "lat"), None),
        ),
        check_vma=False,
    )
```

time: 414 us -> 68.3 us (0.16); the launches traced: 408 us -> 68.1 us
  waiting for transfers between devices: 162 us -> 10.9 us
  matrix products: 89.4 us -> 0 us
  local copies, waits for them, and re-layouts: 76.6 us -> 0.1 us
  other arithmetic: 56.3 us -> 0 us
  Pallas kernels: 0 us -> 39.6 us
  between operations: 14.9 us -> 0.84 us
  starting transfers between devices: 8.93 us -> 16.6 us
    reduce_scatter x2 -> x0, waiting for transfers between devices: 141 us -> none  [the longest x1 106 us: shards(): lax.psum_scatter(qkv_term, ('lon', 'lat'), scatter_dimension=0, tiled=True)]
    dot_general x12 -> x0, matrix products: 89.4 us -> none  [the longest x3 36.1 us: attend(): jnp.einsum('wqhe,wkhe->whqk', queries, keyset, preferred_element_type=jnp...]
    pallas_call x0 -> x11, Pallas kernels: none -> 39.6 us  [call(): pl.pallas_call(kernel, out_shape=out_shape, in_specs=[SMEM] * scalars + i...]
    reduce_sum x5 -> x0, other arithmetic: 39.2 us -> none  [the longest x1 21.1 us: attend(): raised = jnp.exp(scores - highest)]
    convert_element_type x8 -> x0, local copies, waits for them, and re-layouts: 20.9 us -> none  [the longest x3 11 us: shards(): tokens_flat.astype(jnp.float32)]
    slice x12 -> x0, local copies, waits for them, and re-layouts: 17.2 us -> none  [the longest x2 5.35 us: attend(): projected[..., width:2 * width]]
    reshape x4 -> x0, local copies, waits for them, and re-layouts: 14 us -> none  [the longest x1 3.76 us: attend(): return mixture.reshape(wincount, tokens_win, width).astype(jnp.bfloat16)]
    ppermute x8 -> x13, waiting for transfers between devices: 20.7 us -> 10.9 us  [the longest x8 5.49 us: shift(): return lax.ppermute(x, ('lon', 'lat'), pairs)]
  transfers between devices with their start and end apart: 10 -> 13, of which waited for: 7 -> 6; matrix products, arithmetic and copies ran while one was open for 27% -> 0% of each run, Pallas kernels for 0% -> 28%
where the time goes in v1:
time: 68.3 us; the launch traced here: 68.1 us
  Pallas kernels  39.6 us (58%)
  starting transfers between devices  16.6 us (24%)
  waiting for transfers between devices  10.9 us (16%)
  between operations  0.84 us (1%)
    pallas_call x11, Pallas kernels, call(): pl.pallas_call(kernel, out_shape=out_shape, in_specs=[SMEM] * scalars + i...  39.6 us
    ppermute x8, starting transfers between devices, shift(): return lax.ppermute(x, ('lon', 'lat'), pairs)  13.2 us
    ppermute x8, waiting for transfers between devices, shift(): return lax.ppermute(x, ('lon', 'lat'), pairs)  5.49 us
    ppermute x5, waiting for transfers between devices, partner(): lax.ppermute(x, axis, [(i, i ^ flip) for i in range(lax.axis_size(axis))])  5.44 us
    ppermute x5, starting transfers between devices, partner(): lax.ppermute(x, axis, [(i, i ^ flip) for i in range(lax.axis_size(axis))])  3.47 us
  transfers between devices with their start and end apart: 13, of which 6 were waited for; matrix products, arithmetic and copies ran while one was open for 0% of the time, Pallas kernels for 28%

profile of v1, /device:TPU:0, one launch (start us, length us, event | category | flops | bytes accessed | tf_op | source)
XLA Modules:
  0.0 68.1 jit_solution(5287455152648094694)
XLA Ops:
  0.7 2.3 %shard_map.75 = (bf16[2,2,3,24,512]{4,3,2,1,0:T(8,128)(2,1)}, bf16[3,21,8,512]{3,2,1,0:T(8,128)(2,1)S(1)}, bf16[2,2,3,8,512]{4,3,2,1,0:T(8,128)(2,1)}) custom-call(bf16[2,24,24,512]{3,2,1,0:T(8,128)(2,1)} %f_hbm.5, bf16[2,24,24,512]{3,2,1,0:T(8,128)(2,1)} %c_hbm.5), custom_call_target="tpu_custom_call" | custom-call | flops 1000000000 | bytes 2359296 | tf_op jit(solution)/shard_map/pallas_call | solution.py:637
  3.0 6.4 %collective-permute-start.2 = (bf16[2,2,3,8,512]{4,3,2,1,0:T(8,128)(2,1)}, bf16[2,2,3,8,512]{4,3,2,1,0:T(8,128)(2,1)S(1)}, u32[]{:S(2)}, u32[]{:S(2)}) collective-permute-start(bf16[2,2,3,8,512]{4,3,2,1,0:T(8,128)(2,1)} %get-tuple-element.62), channel_id=1, source_target_pairs={{0,31},{1,28},{2,29},{3,30},{4,3},{5,0},{6,1},{7,2},{8,7},{9,4},{1... | collective-permute-start | bytes 294920 | tf_op jit(solution)/shard_map/ppermute | solution.py:662
  9.4 0.4 collective-permute-start
  9.8 0.6 collective-permute-start.1
  10.4 10.4 %shard_map.76 = (bf16[3,144,512]{2,1,0:T(8,128)(2,1)}, bf16[3,144,512]{2,1,0:T(8,128)(2,1)}, bf16[3,144,512]{2,1,0:T(8,128)(2,1)}, bf16[3,144,1536]{2,1,0:T(8,12...) custom-call(bf16[2,24,24,512]{3,2,1,0:T(8,128)(2,1)} %f_hbm.5, bf16[2,24,24,512]{3,2,1,0:T(8,128)(2,1)} %c_hbm.5, ...), custom_call_target="tpu_custom_call" | custom-call | flops 11000000512 | bytes 4456448 | tf_op jit(solution)/shard_map/pallas_call | solution.py:637
  21.0 16.7 %shard_map.77 = (bf16[5,144,512]{2,1,0:T(8,128)(2,1)S(1)}, bf16[5,144,512]{2,1,0:T(8,128)(2,1)S(1)}, bf16[5,144,512]{2,1,0:T(8,128)(2,1)S(1)}, bf16[5,144,1536]{...) custom-call(s32[5]{0:T(128)S(1)} %stack.27.where_ref, ...), custom_call_target="tpu_custom_call" | custom-call | flops 20000000000 | bytes 8019988 | tf_op jit(solution)/shard_map/pallas_call | solution.py:637
  37.8 2.6 %collective-permute-done.3.other_ref = bf16[4,64,2048]{2,1,0:T(8,128)(2,1)S(1)} collective-permute-done((bf16[4,64,2048]{2,1,0:T(8,128)(2,1)S(1)}, bf16[4,64,2048]{2,1,0:T(8,128)(2,1)S(1)}, u32[]{:S(2)}, u32[]{:S(2)}) %collective-permute-start.3) | collective-permute-done | bytes 1048608 | tf_op jit(solution)/shard_map/ppermute | solution.py:666
  40.4 0.8 %shard_map.78 = (bf16[2,64,1024]{2,1,0:T(8,128)(2,1)S(1)}, bf16[2,64,1024]{2,1,0:T(8,128)(2,1)S(1)}, bf16[2,64,1024]{2,1,0:T(8,128)(2,1)S(1)}, bf16[2,64,1024]{2,1,0:T(8,128)(2,1)S(1)}) custom-call(s32[5]{0:T(128)S(1)} %stack.27.where_ref, bf16[4,64,2048]{2,1,0:T(8,128)(2,1)S(1)} %get-tuple-element.67.mine_ref, ...), custom_call_target="tpu_custom_call" | custom-call | flops 1000000000 | bytes 2097172 | tf_op jit(solution)/shard_map/pallas_call | solution.py:637
  41.3 1.1 %collective-permute-start.5 = (bf16[2,64,1024]{2,1,0:T(8,128)(2,1)S(1)}, bf16[2,64,1024]{2,1,0:T(8,128)(2,1)S(1)}, u32[]{:S(2)}, u32[]{:S(2)}) collective-permute-start(bf16[2,64,1024]{2,1,0:T(8,128)(2,1)S(1)} %get-tuple-element.75), channel_id=1, source_target_pairs={{0,16},{4,20},{8,24},{12,28},{16,0},{20,4},{24,8},{28,12},{1,17},{... | collective-permute-start | bytes 786440 | tf_op jit(solution)/shard_map/ppermute | solution.py:666
  42.4 3.1 %shard_map.79 = (bf16[5,144,512]{2,1,0:T(8,128)(2,1)}, bf16[5,144,512]{2,1,0:T(8,128)(2,1)}, bf16[2,2,3,24,512]{4,3,2,1,0:T(8,128)(2,1)S(1)}, bf16[3,21,8,512]{3,2,1,0:T(8,128)(2,1)S(1)}) custom-call(bf16[5,144,512]{2,1,0:T(8,128)(2,1)S(1)} %get-tuple-element.76.x_ref, bf16[5,144,512]{2,1,0:T(8,128)(2,1)S(1)} %get-tuple-element.77.g_ref, ...), custom_call_target="tpu_custom_call" | custom-call | flops 5000000000 | bytes 6520832 | tf_op jit(solution)/shard_map/pallas_call | solution.py:637
  45.5 1.6 %collective-permute-start.8 = (bf16[2,2,3,24,512]{4,3,2,1,0:T(8,128)(2,1)S(1)}, bf16[2,2,3,24,512]{4,3,2,1,0:T(8,128)(2,1)S(1)}, u32[]{:S(2)}, u32[]{:S(2)}) collective-permute-start(bf16[2,2,3,24,512]{4,3,2,1,0:T(8,128)(2,1)S(1)} %get-tuple-element.87), channel_id=1, source_target_pairs={{0,1},{1,2},{2,3},{3,0},{4,5},{5,6},{6,7},{7,4},{8,9},{9,10},{10,1... | collective-permute-start | bytes 884744 | tf_op jit(solution)/shard_map/ppermute | solution.py:662
  47.1 2.5 %collective-permute-done.4.refs_2_ = bf16[2,64,1024]{2,1,0:T(8,128)(2,1)S(1)} collective-permute-done((bf16[2,64,1024]{2,1,0:T(8,128)(2,1)S(1)}, bf16[2,64,1024]{2,1,0:T(8,128)(2,1)S(1)}, u32[]{:S(2)}, u32[]{:S(2)}) %collective-permute-start.4) | collective-permute-done | bytes 262176 | tf_op jit(solution)/shard_map/ppermute | solution.py:666
  49.7 0.7 shard_map.80
  50.4 0.8 %collective-permute-start.6 = (bf16[64,1024]{1,0:T(8,128)(2,1)S(1)}, bf16[64,1024]{1,0:T(8,128)(2,1)S(1)}, u32[]{:S(2)}, u32[]{:S(2)}) collective-permute-start(bf16[64,1024]{1,0:T(8,128)(2,1)S(1)} %get-tuple-element.85), channel_id=1, source_target_pairs={{0,16},{4,20},{8,24},{12,28},{16,0},{20,4},{24,8},{28,12},{1,17},{... | collective-permute-start | bytes 393224 | tf_op jit(solution)/shard_map/ppermute | solution.py:666
  51.2 1.4 %collective-permute-start.7 = (bf16[64,1024]{1,0:T(8,128)(2,1)S(1)}, bf16[64,1024]{1,0:T(8,128)(2,1)S(1)}, u32[]{:S(2)}, u32[]{:S(2)}) collective-permute-start(bf16[64,1024]{1,0:T(8,128)(2,1)S(1)} %get-tuple-element.86), channel_id=1, source_target_pairs={{0,8},{4,12},{8,0},{12,4},{16,24},{20,28},{24,16},{28,20},{1,9},{5... | collective-permute-start | bytes 393224 | tf_op jit(solution)/shard_map/ppermute | solution.py:666
  52.6 3.2 %collective-permute-done.8.lat_ref.refs_4_ = bf16[2,2,3,24,512]{4,3,2,1,0:T(8,128)(2,1)S(1)} collective-permute-done((bf16[2,2,3,24,512]{4,3,2,1,0:T(8,128)(2,1)S(1)}, bf16[2,2,3,24,512]{4,3,2,1,0:T(8,128)(2,1)S(1)}, u32[]{:S(2)}, u32[]{:S(2)}) %collective-permute-start.8) | collective-permute-done | bytes 294944 | tf_op jit(solution)/shard_map/ppermute | solution.py:662
  56.1 0.6 shard_map.82
  56.8 1.6 %collective-permute-start.9 = (bf16[16,2048]{1,0:T(8,128)(2,1)S(1)}, bf16[16,2048]{1,0:T(8,128)(2,1)S(1)}, u32[]{:S(2)}, u32[]{:S(2)}) collective-permute-start(bf16[16,2048]{1,0:T(8,128)(2,1)S(1)} %get-tuple-element.96), channel_id=1, source_target_pairs={{0,1},{1,2},{2,3},{3,0},{4,5},{5,6},{6,7},{7,4},{8,9},{9,10},{10,1... | collective-permute-start | bytes 196616 | tf_op jit(solution)/shard_map/ppermute | solution.py:662
  58.4 1.4 %collective-permute-start.10 = (bf16[16,2048]{1,0:T(8,128)(2,1)S(1)}, bf16[16,2048]{1,0:T(8,128)(2,1)S(1)}, u32[]{:S(2)}, u32[]{:S(2)}) collective-permute-start(bf16[16,2048]{1,0:T(8,128)(2,1)S(1)} %get-tuple-element.97), channel_id=1, source_target_pairs={{0,2},{1,3},{2,0},{3,1},{4,6},{5,7},{6,4},{7,5},{8,10},{9,11},{10,... | collective-permute-start | bytes 196616 | tf_op jit(solution)/shard_map/ppermute | solution.py:662
  59.8 1.1 %collective-permute-start.11 = (bf16[16,2048]{1,0:T(8,128)(2,1)S(1)}, bf16[16,2048]{1,0:T(8,128)(2,1)S(1)}, u32[]{:S(2)}, u32[]{:S(2)}) collective-permute-start(bf16[16,2048]{1,0:T(8,128)(2,1)S(1)} %get-tuple-element.98), channel_id=1, source_target_pairs={{0,3},{1,0},{2,1},{3,2},{4,7},{5,4},{6,5},{7,6},{8,11},{9,8},{10,9... | collective-permute-start | bytes 196616 | tf_op jit(solution)/shard_map/ppermute | solution.py:662
  60.8 3.0 %shard_map.83 = (bf16[2,24,24,512]{3,2,1,0:T(8,128)(2,1)}, bf16[2,24,24,512]{3,2,1,0:T(8,128)(2,1)}, bf16[2,2,24,16,512]{4,3,2,1,0:T(8,128)(2,1)S(1)}) custom-call(bf16[3,144,512]{2,1,0:T(8,128)(2,1)} %get-tuple-element.99.refs_0_, bf16[5,144,512]{2,1,0:T(8,128)(2,1)} %get-tuple-element.100.refs_1_, bf16[3,144,512]{2,1,0:T(8,128)(2,1)} %get-tuple-element.101.refs_2_, ...), custom_call_target="tpu_custom_call" | custom-call | flops 4000000000 | bytes 2654208 | tf_op jit(solution)/shard_map/pallas_call | solution.py:637
  63.9 2.3 %collective-permute-done.12.lon_ref = bf16[3,24,8,512]{3,2,1,0:T(8,128)(2,1)S(1)} collective-permute-done((bf16[3,24,8,512]{3,2,1,0:T(8,128)(2,1)S(1)}, bf16[3,24,8,512]{3,2,1,0:T(8,128)(2,1)S(1)}, u32[]{:S(2)}, u32[]{:S(2)}) %collective-permute-start.12) | collective-permute-done | bytes 589856 | tf_op jit(solution)/shard_map/ppermute | solution.py:662
  66.1 1.3 %shard_map.84 = (bf16[2,24,24,512]{3,2,1,0:T(8,128)(2,1)}, bf16[2,24,24,512]{3,2,1,0:T(8,128)(2,1)}) custom-call(bf16[2,2,24,16,512]{4,3,2,1,0:T(8,128)(2,1)S(1)} %get-tuple-element.103.left_ref, bf16[3,24,8,512]{3,2,1,0:T(8,128)(2,1)S(1)} %collective-permute-done.12.lon_ref, ...), custom_call_target="tpu_custom_call", output_to_operand_aliasing={{0}: (2, {}), {1}: (3, {})} | custom-call | flops 2000000000 | bytes 4521984 | tf_op jit(solution)/shard_map/pallas_call | solution.py:637
  67.4 0.7 shard_map.85
  (20 shorter events, 0.6 us)
Async XLA Ops:
  0.6 9.8 %copy-start.1 = (bf16[512,512]{1,0:T(8,128)(2,1)S(1)}, bf16[512,512]{1,0:T(8,128)(2,1)}, u32[]{:S(2)}) copy-start(bf16[512,512]{1,0:T(8,128)(2,1)} %wo_ref.3) | copy-start | bytes 1572868
  0.6 9.8 %copy-start = (bf16[512,1536]{1,0:T(8,128)(2,1)S(1)}, bf16[512,1536]{1,0:T(8,128)(2,1)}, u32[]{:S(2)}) copy-start(bf16[512,1536]{1,0:T(8,128)(2,1)} %w_ref.5) | copy-start | bytes 4718596
  3.0 18.0 %collective-permute-start.2 = (bf16[2,2,3,8,512]{4,3,2,1,0:T(8,128)(2,1)}, bf16[2,2,3,8,512]{4,3,2,1,0:T(8,128)(2,1)S(1)}, u32[]{:S(2)}, u32[]{:S(2)}) collective-permute-start(bf16[2,2,3,8,512]{4,3,2,1,0:T(8,128)(2,1)} %get-tuple-element.62), channel_id=1, source_target_pairs={{0,31},{1,28},{2,29},{3,30},{4,3},{5,0},{6,1},{7,2},{8,7},{9,4},{1... | collective-permute-start | bytes 294920 | tf_op jit(solution)/shard_map/ppermute | solution.py:662
  9.4 11.6 %collective-permute-start = (bf16[2,2,3,24,512]{4,3,2,1,0:T(8,128)(2,1)}, bf16[2,2,3,24,512]{4,3,2,1,0:T(8,128)(2,1)S(1)}, u32[]{:S(2)}, u32[]{:S(2)}) collective-permute-start(bf16[2,2,3,24,512]{4,3,2,1,0:T(8,128)(2,1)} %get-tuple-element.60), channel_id=1, source_target_pairs={{0,3},{1,0},{2,1},{3,2},{4,7},{5,4},{6,5},{7,6},{8,11},{9,8},{10,9... | collective-permute-start | bytes 884744 | tf_op jit(solution)/shard_map/ppermute | solution.py:662
  9.8 11.1 %collective-permute-start.1 = (bf16[3,21,8,512]{3,2,1,0:T(8,128)(2,1)S(1)}, bf16[3,21,8,512]{3,2,1,0:T(8,128)(2,1)S(1)}, u32[]{:S(2)}, u32[]{:S(2)}) collective-permute-start(bf16[3,21,8,512]{3,2,1,0:T(8,128)(2,1)S(1)} %get-tuple-element.61), channel_id=1, source_target_pairs={{0,28},{1,29},{2,30},{3,31},{4,0},{5,1},{6,2},{7,3},{8,4},{9,5},{1... | collective-permute-start | bytes 1548296 | tf_op jit(solution)/shard_map/ppermute | solution.py:662
  37.7 2.7 %collective-permute-start.3 = (bf16[4,64,2048]{2,1,0:T(8,128)(2,1)S(1)}, bf16[4,64,2048]{2,1,0:T(8,128)(2,1)S(1)}, u32[]{:S(2)}, u32[]{:S(2)}) collective-permute-start(bf16[4,64,2048]{2,1,0:T(8,128)(2,1)S(1)} %get-tuple-element.68), channel_id=1, source_target_pairs={{0,4},{4,0},{8,12},{12,8},{16,20},{20,16},{24,28},{28,24},{1,5},{5... | collective-permute-start | bytes 3145736 | tf_op jit(solution)/shard_map/ppermute | solution.py:666
  40.4 2.0 %copy-start.2 = (bf16[512,512]{1,0:T(8,128)(2,1)S(1)}, bf16[512,512]{1,0:T(8,128)(2,1)}, u32[]{:S(2)}) copy-start(bf16[512,512]{1,0:T(8,128)(2,1)} %wo_ref.3) | copy-start | bytes 1572868
  41.2 8.4 %collective-permute-start.4 = (bf16[2,64,1024]{2,1,0:T(8,128)(2,1)S(1)}, bf16[2,64,1024]{2,1,0:T(8,128)(2,1)S(1)}, u32[]{:S(2)}, u32[]{:S(2)}) collective-permute-start(bf16[2,64,1024]{2,1,0:T(8,128)(2,1)S(1)} %get-tuple-element.74), channel_id=1, source_target_pairs={{0,8},{4,12},{8,0},{12,4},{16,24},{20,28},{24,16},{28,20},{1,9},{5... | collective-permute-start | bytes 786440 | tf_op jit(solution)/shard_map/ppermute | solution.py:666
  41.3 8.4 %collective-permute-start.5 = (bf16[2,64,1024]{2,1,0:T(8,128)(2,1)S(1)}, bf16[2,64,1024]{2,1,0:T(8,128)(2,1)S(1)}, u32[]{:S(2)}, u32[]{:S(2)}) collective-permute-start(bf16[2,64,1024]{2,1,0:T(8,128)(2,1)S(1)} %get-tuple-element.75), channel_id=1, source_target_pairs={{0,16},{4,20},{8,24},{12,28},{16,0},{20,4},{24,8},{28,12},{1,17},{... | collective-permute-start | bytes 786440 | tf_op jit(solution)/shard_map/ppermute | solution.py:666
  45.5 10.4 %collective-permute-start.8 = (bf16[2,2,3,24,512]{4,3,2,1,0:T(8,128)(2,1)S(1)}, bf16[2,2,3,24,512]{4,3,2,1,0:T(8,128)(2,1)S(1)}, u32[]{:S(2)}, u32[]{:S(2)}) collective-permute-start(bf16[2,2,3,24,512]{4,3,2,1,0:T(8,128)(2,1)S(1)} %get-tuple-element.87), channel_id=1, source_target_pairs={{0,1},{1,2},{2,3},{3,0},{4,5},{5,6},{6,7},{7,4},{8,9},{9,10},{10,1... | collective-permute-start | bytes 884744 | tf_op jit(solution)/shard_map/ppermute | solution.py:662
  50.4 5.6 %collective-permute-start.6 = (bf16[64,1024]{1,0:T(8,128)(2,1)S(1)}, bf16[64,1024]{1,0:T(8,128)(2,1)S(1)}, u32[]{:S(2)}, u32[]{:S(2)}) collective-permute-start(bf16[64,1024]{1,0:T(8,128)(2,1)S(1)} %get-tuple-element.85), channel_id=1, source_target_pairs={{0,16},{4,20},{8,24},{12,28},{16,0},{20,4},{24,8},{28,12},{1,17},{... | collective-permute-start | bytes 393224 | tf_op jit(solution)/shard_map/ppermute | solution.py:666
  51.2 5.0 %collective-permute-start.7 = (bf16[64,1024]{1,0:T(8,128)(2,1)S(1)}, bf16[64,1024]{1,0:T(8,128)(2,1)S(1)}, u32[]{:S(2)}, u32[]{:S(2)}) collective-permute-start(bf16[64,1024]{1,0:T(8,128)(2,1)S(1)} %get-tuple-element.86), channel_id=1, source_target_pairs={{0,8},{4,12},{8,0},{12,4},{16,24},{20,28},{24,16},{28,20},{1,9},{5... | collective-permute-start | bytes 393224 | tf_op jit(solution)/shard_map/ppermute | solution.py:666
  55.9 10.3 %collective-permute-start.12 = (bf16[3,24,8,512]{3,2,1,0:T(8,128)(2,1)S(1)}, bf16[3,24,8,512]{3,2,1,0:T(8,128)(2,1)S(1)}, u32[]{:S(2)}, u32[]{:S(2)}) collective-permute-start(bf16[3,24,8,512]{3,2,1,0:T(8,128)(2,1)S(1)} %shard_map.81), channel_id=1, source_target_pairs={{0,4},{1,5},{2,6},{3,7},{4,8},{5,9},{6,10},{7,11},{8,12},{9,13},{1... | collective-permute-start | bytes 1769480 | tf_op jit(solution)/shard_map/ppermute | solution.py:662
  56.8 10.6 %collective-permute-start.9 = (bf16[16,2048]{1,0:T(8,128)(2,1)S(1)}, bf16[16,2048]{1,0:T(8,128)(2,1)S(1)}, u32[]{:S(2)}, u32[]{:S(2)}) collective-permute-start(bf16[16,2048]{1,0:T(8,128)(2,1)S(1)} %get-tuple-element.96), channel_id=1, source_target_pairs={{0,1},{1,2},{2,3},{3,0},{4,5},{5,6},{6,7},{7,4},{8,9},{9,10},{10,1... | collective-permute-start | bytes 196616 | tf_op jit(solution)/shard_map/ppermute | solution.py:662
  58.4 9.0 %collective-permute-start.10 = (bf16[16,2048]{1,0:T(8,128)(2,1)S(1)}, bf16[16,2048]{1,0:T(8,128)(2,1)S(1)}, u32[]{:S(2)}, u32[]{:S(2)}) collective-permute-start(bf16[16,2048]{1,0:T(8,128)(2,1)S(1)} %get-tuple-element.97), channel_id=1, source_target_pairs={{0,2},{1,3},{2,0},{3,1},{4,6},{5,7},{6,4},{7,5},{8,10},{9,11},{10,... | collective-permute-start | bytes 196616 | tf_op jit(solution)/shard_map/ppermute | solution.py:662
  59.8 7.6 %collective-permute-start.11 = (bf16[16,2048]{1,0:T(8,128)(2,1)S(1)}, bf16[16,2048]{1,0:T(8,128)(2,1)S(1)}, u32[]{:S(2)}, u32[]{:S(2)}) collective-permute-start(bf16[16,2048]{1,0:T(8,128)(2,1)S(1)} %get-tuple-element.98), channel_id=1, source_target_pairs={{0,3},{1,0},{2,1},{3,2},{4,7},{5,4},{6,5},{7,6},{8,11},{9,8},{10,9... | collective-permute-start | bytes 196616 | tf_op jit(solution)/shard_map/ppermute | solution.py:662
